TPU v7x, 32 devices: a whole 2x2x4 slice. The times are simulated.
32 devices in a mesh: section: 4 (over y, x), dp: 8 (over z, core).
Axes of the slice: x: 2, y: 2, z: 4, core: 2. Of those that a mesh axis runs over, the one named last changes fastest.
Arguments:
- inputs: bfloat16 [4, 256, 2048], P(None, 'dp'), may hold values from -6 to 6
- route: int32 [4, 4, 256, 6], P('section', None, 'dp'), may hold values from 0 to 7, as said below
- gain: bfloat16 [4, 2048], P('section'), may hold values from 0.099609375 to 1.8984375
- router: bfloat16 [4, 2048, 8], P('section'), may hold values from -0.125 to 0.125
- w_gate: bfloat16 [4, 8, 2048, 768], P('section', 'dp'), may hold values from -0.125 to 0.125
- w_up: bfloat16 [4, 8, 2048, 768], P('section', 'dp'), may hold values from -0.125 to 0.125
- w_down: bfloat16 [4, 8, 768, 2048], P('section', 'dp'), may hold values from -0.21875 to 0.21875
Outputs:
- states: bfloat16 [4, 4, 256, 2048], P('section', None, 'dp')
Inputs may be any that keep to these rules, and one draw needn't show every extreme that they name: `route`: each token names 6 different experts. Among the 32 tokens of one index of dp in one micro-batch and layer, no expert is named more than 32 times; in every micro-batch and layer one expert is named exactly 32 times by the tokens of every index of dp.
All inputs are finite; a program needn't handle non-finite values.
Results may differ from a plain program's by a relative error of at most 0.015.
Values may be sent and summed in bfloat16 or wider, within the bound.
A program may use at most 128 MiB of HBM per device.

v0:
```python
import jax
import jax.numpy as jnp
from jax import lax
from jax.sharding import PartitionSpec as P

EPS = 1e-06


def shifted(x, axis, by):
    devices = lax.axis_size(axis)
    pairs = [(i, i + by) for i in range(devices) if 0 <= i + by < devices]
    return lax.ppermute(x, axis, pairs)


def expert_rows(rows, gate_mat, up_mat, down_mat):
    gate_act = jnp.dot(rows, gate_mat, preferred_element_type=jnp.float32)
    up_act = jnp.dot(rows, up_mat, preferred_element_type=jnp.float32)
    hidden = (jax.nn.silu(gate_act) * up_act).astype(jnp.bfloat16)
    return jnp.dot(hidden, down_mat, preferred_element_type=jnp.float32).astype(jnp.bfloat16)


def on_device(inputs, route, gain, router, w_gate, w_up, w_down):
    section_count = lax.axis_size("section")
    section_index = lax.axis_index("section")
    micro_count, tok_rows, model_width = inputs.shape
    top_count = route.shape[-1]
    experts = router.shape[-1]
    pair_load = 2 * tok_rows * top_count // experts
    capacity = min(pair_load, tok_rows)
    slot_count = experts * capacity
    gate_mat = w_gate[0, 0]
    up_mat = w_up[0, 0]
    down_mat = w_down[0, 0]
    gain_row = gain[0].astype(jnp.float32)
    router_mat = router[0]
    expert_ids = jnp.arange(experts, dtype=jnp.int32)
    slot_ids = jnp.arange(slot_count, dtype=jnp.int32)

    def compute_all(flat_rows):
        return expert_rows(flat_rows, gate_mat, up_mat, down_mat)

    def skip_all(flat_rows):
        return jnp.zeros_like(flat_rows)

    inbound = jnp.zeros((tok_rows, model_width), jnp.bfloat16)
    states = jnp.zeros((micro_count, tok_rows, model_width), jnp.bfloat16)
    for tick_no in range(micro_count + section_count - 1):
        micro_now = tick_no - section_index
        active = (micro_now >= 0) & (micro_now < micro_count)
        micro_index = jnp.clip(micro_now, 0, micro_count - 1)
        fresh_rows = lax.dynamic_index_in_dim(inputs, micro_index, 0, keepdims=False)
        current = jnp.where(section_index == 0, fresh_rows, inbound)
        chosen_ids = lax.dynamic_index_in_dim(route[0], micro_index, 0, keepdims=False)
        wide_state = current.astype(jnp.float32)
        inv_rms = lax.rsqrt(jnp.mean(wide_state * wide_state, axis=1, keepdims=True) + EPS)
        normed = (wide_state * inv_rms * gain_row).astype(jnp.bfloat16)
        logits = jnp.dot(normed, router_mat, preferred_element_type=jnp.float32)
        scores = jax.nn.sigmoid(jnp.take_along_axis(logits, chosen_ids, axis=1))
        weights = scores / jnp.sum(scores, axis=1, keepdims=True)
        flat_ids = chosen_ids.reshape(-1)
        onehot = (flat_ids[:, None] == expert_ids[None, :]).astype(jnp.int32)
        slot_rank = jnp.sum((jnp.cumsum(onehot, axis=0) - onehot) * onehot, axis=1)
        target = flat_ids * capacity + slot_rank
        selector = (target[None, :] == slot_ids[:, None]) & active
        by_token = jnp.sum(
            selector.reshape(slot_count, tok_rows, top_count).astype(jnp.int32), axis=2
        )
        buffer = jnp.dot(
            by_token.astype(jnp.bfloat16), normed, preferred_element_type=jnp.float32
        ).astype(jnp.bfloat16)
        live_slots = jnp.sum(by_token, axis=1).reshape(experts, capacity)
        slot_buffer = buffer.reshape(experts, capacity, model_width)
        slot_rows = lax.all_to_all(slot_buffer, "dp", split_axis=0, concat_axis=0, tiled=True)
        slot_live = lax.all_to_all(live_slots, "dp", split_axis=0, concat_axis=0, tiled=True)
        source_count, item_count = slot_live.shape
        row_count = source_count * item_count
        run_flat_rows = slot_rows.reshape(row_count, model_width)
        live_flat = slot_live.reshape(row_count)
        expert_out = lax.cond(jnp.any(live_flat > 0), compute_all, skip_all, run_flat_rows)
        expert_out = expert_out.reshape(source_count, item_count, model_width)
        returned = lax.all_to_all(expert_out, "dp", split_axis=0, concat_axis=0, tiled=True)
        copies = returned.reshape(slot_count, model_width)[target].reshape(
            tok_rows, top_count, model_width
        )
        mixed = jnp.einsum("tk,tkd->td", weights, copies.astype(jnp.float32))
        layer_out = (wide_state + mixed).astype(jnp.bfloat16)
        previous = lax.dynamic_index_in_dim(states, micro_index, 0, keepdims=False)
        states = lax.dynamic_update_index_in_dim(
            states, jnp.where(active, layer_out, previous), micro_index, 0
        )
        inbound = shifted(layer_out, "section", 1)
    return states[None]


def solution(mesh):
    in_specs = (
        P(None, "dp", None),
        P("section", None, "dp", None),
        P("section", None),
        P("section", None, None),
        P("section", "dp", None, None),
        P("section", "dp", None, None),
        P("section", "dp", None, None),
    )
    out_specs = P("section", None, "dp", None)
    return jax.shard_map(
        on_device, mesh=mesh, in_specs=in_specs, out_specs=out_specs, check_vma=False
    )
```

profile of v0, /device:TPU:6, one launch (start us, length us, event | category | flops | bytes accessed | tf_op | source)
XLA Modules:
  0.0 569.4 jit_solution(7181878200754794126)
XLA Ops:
  3.2 4.9 all-to-all-start
  13.5 3.8 all-to-all-start.1
  20.5 23.4 %all-to-all-done.1 = bf16[8,32,2048]{2,1,0:T(8,128)(2,1)S(1)} async-done(((bf16[8,32,2048]{2,1,0:T(8,128)(2,1)}), bf16[8,32,2048]{2,1,0:T(8,128)(2,1)S(1)}, u32[]{:S(2)}, u32[]{:S(2)}) %all-to-all-start.1) | async-done | bytes 1048608 | tf_op jit(solution)/shard_map/all_to_all | solution.py:73
  45.0 3.6 all-to-all-start.2
  51.4 23.7 %all-to-all-done.2 = bf16[8,32,2048]{2,1,0:T(8,128)(2,1)S(1)} async-done(((bf16[8,32,2048]{2,1,0:T(8,128)(2,1)}), bf16[8,32,2048]{2,1,0:T(8,128)(2,1)S(1)}, u32[]{:S(2)}, u32[]{:S(2)}) %all-to-all-start.2) | async-done | bytes 1048608 | tf_op jit(solution)/shard_map/all_to_all | solution.py:81
  79.2 3.3 all-to-all-start.3
  88.0 3.6 all-to-all-start.4
  92.8 25.2 %all-to-all-done.4 = bf16[8,32,2048]{2,1,0:T(8,128)(2,1)S(1)} async-done(((bf16[8,32,2048]{2,1,0:T(8,128)(2,1)}), bf16[8,32,2048]{2,1,0:T(8,128)(2,1)S(1)}, u32[]{:S(2)}, u32[]{:S(2)}) %all-to-all-start.4) | async-done | bytes 1048608 | tf_op jit(solution)/shard_map/all_to_all | solution.py:73
  119.1 3.7 all-to-all-start.5
  125.3 24.0 %all-to-all-done.5 = bf16[8,32,2048]{2,1,0:T(8,128)(2,1)S(1)} async-done(((bf16[8,32,2048]{2,1,0:T(8,128)(2,1)}), bf16[8,32,2048]{2,1,0:T(8,128)(2,1)S(1)}, u32[]{:S(2)}, u32[]{:S(2)}) %all-to-all-start.5) | async-done | bytes 1048608 | tf_op jit(solution)/shard_map/all_to_all | solution.py:81
  153.5 3.3 all-to-all-start.6
  162.2 3.6 all-to-all-start.7
  168.3 24.0 %all-to-all-done.7 = bf16[8,32,2048]{2,1,0:T(8,128)(2,1)S(1)} async-done(((bf16[8,32,2048]{2,1,0:T(8,128)(2,1)}), bf16[8,32,2048]{2,1,0:T(8,128)(2,1)S(1)}, u32[]{:S(2)}, u32[]{:S(2)}) %all-to-all-start.7) | async-done | bytes 1048608 | tf_op jit(solution)/shard_map/all_to_all | solution.py:73
  193.4 3.6 all-to-all-start.8
  200.4 23.0 %all-to-all-done.8 = bf16[8,32,2048]{2,1,0:T(8,128)(2,1)S(1)} async-done(((bf16[8,32,2048]{2,1,0:T(8,128)(2,1)}), bf16[8,32,2048]{2,1,0:T(8,128)(2,1)S(1)}, u32[]{:S(2)}, u32[]{:S(2)}) %all-to-all-start.8) | async-done | bytes 1048608 | tf_op jit(solution)/shard_map/all_to_all | solution.py:81
  227.5 3.3 all-to-all-start.9
  230.9 17.0 %collective-permute-done.2 = bf16[32,2048]{1,0:T(8,128)(2,1)S(1)} collective-permute-done((bf16[32,2048]{1,0:T(8,128)(2,1)S(1)}, bf16[32,2048]{1,0:T(8,128)(2,1)S(1)}, u32[]{:S(2)}, u32[]{:S(2)}) %collective-permute-start.2) | collective-permute-done | bytes 131104 | tf_op jit(solution)/shard_map/ppermute | solution.py:12
  249.5 3.6 all-to-all-start.10
  254.3 25.2 %all-to-all-done.10 = bf16[8,32,2048]{2,1,0:T(8,128)(2,1)S(1)} async-done(((bf16[8,32,2048]{2,1,0:T(8,128)(2,1)}), bf16[8,32,2048]{2,1,0:T(8,128)(2,1)S(1)}, u32[]{:S(2)}, u32[]{:S(2)}) %all-to-all-start.10) | async-done | bytes 1048608 | tf_op jit(solution)/shard_map/all_to_all | solution.py:73
  279.6 8.9 %conditional.10 = (bf16[256,2048]{1,0:T(8,128)(2,1)}) conditional(s32[]{:T(128)} %convert_element_type.269, () %tuple.54, (bf16[8,32,2048]{2,1,0:T(8,128)(2,1)S(1)}, bf16[2048,768]{1,0:T(8,128)(2,1)}, bf16[2048,768]{1,0:T(8,128)(2,1)}, bf16[768,2048]{1,0:T(8,128)(2,1)}) %tuple.127), branch_computations={%region_38.40_spmd, %region_39.41_spmd} | conditional | flops 2417623040 | bytes 14155784 | solution.py:79
  282.4 6.0 %convolution_convert_fusion.3 = bf16[256,2048]{1,0:T(8,128)(2,1)} fusion(bf16[768,2048]{1,0:T(8,128)(2,1)} %get-tuple-element.105, bf16[256,2048]{1,0:T(8,128)(2,1)S(1)} %bitcast.462, bf16[2048,768]{1,0:T(8,128)(2,1)} %get-tuple-element.104, f32[256,768]{1,0:T(8,128)S(1)} %fusion.159), kind=kOutput, calls=%fused_computation.29 | convolution fusion | flops 1612316672 | bytes 9175040 | tf_op jit(solution)/shard_map/cond/branch_1_fun/dot_general | solution.py:19
  288.4 3.8 all-to-all-start.11
  294.7 24.1 %all-to-all-done.11 = bf16[8,32,2048]{2,1,0:T(8,128)(2,1)S(1)} async-done(((bf16[8,32,2048]{2,1,0:T(8,128)(2,1)}), bf16[8,32,2048]{2,1,0:T(8,128)(2,1)S(1)}, u32[]{:S(2)}, u32[]{:S(2)}) %all-to-all-start.11) | async-done | bytes 1048608 | tf_op jit(solution)/shard_map/all_to_all | solution.py:81
  322.8 3.3 all-to-all-start.12
  326.1 4.4 collective-permute-done.3
  332.2 3.6 all-to-all-start.13
  338.2 24.0 %all-to-all-done.13 = bf16[8,32,2048]{2,1,0:T(8,128)(2,1)S(1)} async-done(((bf16[8,32,2048]{2,1,0:T(8,128)(2,1)}), bf16[8,32,2048]{2,1,0:T(8,128)(2,1)S(1)}, u32[]{:S(2)}, u32[]{:S(2)}) %all-to-all-start.13) | async-done | bytes 1048608 | tf_op jit(solution)/shard_map/all_to_all | solution.py:73
  362.2 8.9 %conditional.11 = (bf16[256,2048]{1,0:T(8,128)(2,1)}) conditional(s32[]{:T(128)} %convert_element_type.277, () %tuple.56, (bf16[8,32,2048]{2,1,0:T(8,128)(2,1)S(1)}, bf16[2048,768]{1,0:T(8,128)(2,1)}, bf16[2048,768]{1,0:T(8,128)(2,1)}, bf16[768,2048]{1,0:T(8,128)(2,1)}) %tuple.128), branch_computations={%region_48.50_spmd, %region_49.51_spmd} | conditional | flops 2417623040 | bytes 14155784 | solution.py:79
  362.2 2.9 fusion.160
  365.1 6.0 %convolution_convert_fusion.4 = bf16[256,2048]{1,0:T(8,128)(2,1)} fusion(bf16[768,2048]{1,0:T(8,128)(2,1)} %get-tuple-element.109, bf16[256,2048]{1,0:T(8,128)(2,1)S(1)} %bitcast.456, bf16[2048,768]{1,0:T(8,128)(2,1)} %get-tuple-element.108, f32[256,768]{1,0:T(8,128)S(1)} %fusion.160), kind=kOutput, calls=%fused_computation.34 | convolution fusion | flops 1612316672 | bytes 9175040 | tf_op jit(solution)/shard_map/cond/branch_1_fun/dot_general | solution.py:19
  371.1 3.6 all-to-all-start.14
  378.2 23.0 %all-to-all-done.14 = bf16[8,32,2048]{2,1,0:T(8,128)(2,1)S(1)} async-done(((bf16[8,32,2048]{2,1,0:T(8,128)(2,1)}), bf16[8,32,2048]{2,1,0:T(8,128)(2,1)S(1)}, u32[]{:S(2)}, u32[]{:S(2)}) %all-to-all-start.14) | async-done | bytes 1048608 | tf_op jit(solution)/shard_map/all_to_all | solution.py:81
  405.3 3.3 all-to-all-start.15
  408.6 4.4 collective-permute-done.4
  414.7 3.6 all-to-all-start.16
  419.5 25.2 %all-to-all-done.16 = bf16[8,32,2048]{2,1,0:T(8,128)(2,1)S(1)} async-done(((bf16[8,32,2048]{2,1,0:T(8,128)(2,1)}), bf16[8,32,2048]{2,1,0:T(8,128)(2,1)S(1)}, u32[]{:S(2)}, u32[]{:S(2)}) %all-to-all-start.16) | async-done | bytes 1048608 | tf_op jit(solution)/shard_map/all_to_all | solution.py:73
  444.7 9.1 %conditional.12 = (bf16[256,2048]{1,0:T(8,128)(2,1)}) conditional(s32[]{:T(128)} %convert_element_type.285, () %tuple.58, (bf16[8,32,2048]{2,1,0:T(8,128)(2,1)S(1)}, bf16[2048,768]{1,0:T(8,128)(2,1)}, bf16[2048,768]{1,0:T(8,128)(2,1)}, bf16[768,2048]{1,0:T(8,128)(2,1)}) %tuple.129), branch_computations={%region_58.60_spmd, %region_59.61_spmd} | conditional | flops 2417623040 | bytes 14155784 | solution.py:79
  447.9 6.0 %convolution_convert_fusion.5 = bf16[256,2048]{1,0:T(8,128)(2,1)} fusion(bf16[768,2048]{1,0:T(8,128)(2,1)} %get-tuple-element.113, bf16[256,2048]{1,0:T(8,128)(2,1)S(1)} %bitcast.464, bf16[2048,768]{1,0:T(8,128)(2,1)} %get-tuple-element.112, f32[256,768]{1,0:T(8,128)S(1)} %fusion.161), kind=kOutput, calls=%fused_computation.39 | convolution fusion | flops 1612316672 | bytes 9175040 | tf_op jit(solution)/shard_map/cond/branch_1_fun/dot_general | solution.py:19
  453.9 3.6 all-to-all-start.17
  459.9 24.1 %all-to-all-done.17 = bf16[8,32,2048]{2,1,0:T(8,128)(2,1)S(1)} async-done(((bf16[8,32,2048]{2,1,0:T(8,128)(2,1)}), bf16[8,32,2048]{2,1,0:T(8,128)(2,1)S(1)}, u32[]{:S(2)}, u32[]{:S(2)}) %all-to-all-start.17) | async-done | bytes 1048608 | tf_op jit(solution)/shard_map/all_to_all | solution.py:81
  488.0 3.3 all-to-all-start.18
  491.3 4.4 collective-permute-done.5
  497.4 3.6 all-to-all-start.19
  502.2 25.2 %all-to-all-done.19 = bf16[8,32,2048]{2,1,0:T(8,128)(2,1)S(1)} async-done(((bf16[8,32,2048]{2,1,0:T(8,128)(2,1)}), bf16[8,32,2048]{2,1,0:T(8,128)(2,1)S(1)}, u32[]{:S(2)}, u32[]{:S(2)}) %all-to-all-start.19) | async-done | bytes 1048608 | tf_op jit(solution)/shard_map/all_to_all | solution.py:73
  527.5 8.8 %conditional.13 = (bf16[256,2048]{1,0:T(8,128)(2,1)}) conditional(s32[]{:T(128)} %convert_element_type.293, () %tuple.60, (bf16[8,32,2048]{2,1,0:T(8,128)(2,1)S(1)}, bf16[2048,768]{1,0:T(8,128)(2,1)}, bf16[2048,768]{1,0:T(8,128)(2,1)}, bf16[768,2048]{1,0:T(8,128)(2,1)}) %tuple.130), branch_computations={%region_68.70_spmd, %region_69.71_spmd} | conditional | flops 2417623040 | bytes 14155784 | solution.py:79
  530.3 6.0 %convolution_convert_fusion.6 = bf16[256,2048]{1,0:T(8,128)(2,1)} fusion(bf16[768,2048]{1,0:T(8,128)(2,1)} %get-tuple-element.117, bf16[256,2048]{1,0:T(8,128)(2,1)S(1)} %bitcast.466, bf16[2048,768]{1,0:T(8,128)(2,1)} %get-tuple-element.116, f32[256,768]{1,0:T(8,128)S(1)} %fusion.162), kind=kOutput, calls=%fused_computation.44 | convolution fusion | flops 1612316672 | bytes 9175040 | tf_op jit(solution)/shard_map/cond/branch_1_fun/dot_general | solution.py:19
  536.3 3.6 all-to-all-start.20
  542.9 23.5 %all-to-all-done.20 = bf16[8,32,2048]{2,1,0:T(8,128)(2,1)S(1)} async-done(((bf16[8,32,2048]{2,1,0:T(8,128)(2,1)}), bf16[8,32,2048]{2,1,0:T(8,128)(2,1)S(1)}, u32[]{:S(2)}, u32[]{:S(2)}) %all-to-all-start.20) | async-done | bytes 1048608 | tf_op jit(solution)/shard_map/all_to_all | solution.py:81
  (294 shorter events, 96.5 us)
Async XLA Ops:
  0.0 17.5 %copy-start = (bf16[1,2048,8]{1,2,0:T(8,128)(2,1)S(1)}, bf16[1,2048,8]{1,2,0:T(8,128)(2,1)}, u32[]{:S(2)}) copy-start(bf16[1,2048,8]{1,2,0:T(8,128)(2,1)} %param.26) | copy-start | bytes 98308
  0.0 17.5 %copy-start.1 = (bf16[4,32,2048]{2,1,0:T(8,128)(2,1)S(1)}, bf16[4,32,2048]{2,1,0:T(8,128)(2,1)}, u32[]{:S(2)}) copy-start(bf16[4,32,2048]{2,1,0:T(8,128)(2,1)} %param.23) | copy-start | bytes 1572868
  3.2 10.4 %all-to-all-start = ((s32[8,1,32]{2,1,0:T(1,128)}), s32[8,1,32]{2,1,0:T(1,128)S(1)}, u32[]{:S(2)}, u32[]{:S(2)}) async-start(s32[8,1,32]{2,1,0:T(1,128)} %all_to_all.84), calls=%async_computation | async-start | bytes 8192 | tf_op jit(solution)/shard_map/all_to_all | solution.py:74
  13.5 30.4 %all-to-all-start.1 = ((bf16[8,32,2048]{2,1,0:T(8,128)(2,1)}), bf16[8,32,2048]{2,1,0:T(8,128)(2,1)S(1)}, u32[]{:S(2)}, u32[]{:S(2)}) async-start(bf16[8,32,2048]{2,1,0:T(8,128)(2,1)} %bitcast.18), calls=%async_computation.1 | async-start | bytes 2097152 | tf_op jit(solution)/shard_map/all_to_all | solution.py:73
  45.0 30.1 %all-to-all-start.2 = ((bf16[8,32,2048]{2,1,0:T(8,128)(2,1)}), bf16[8,32,2048]{2,1,0:T(8,128)(2,1)S(1)}, u32[]{:S(2)}, u32[]{:S(2)}) async-start(bf16[8,32,2048]{2,1,0:T(8,128)(2,1)} %bitcast.22), calls=%async_computation.2 | async-start | bytes 2097152 | tf_op jit(solution)/shard_map/all_to_all | solution.py:81
  77.1 6.9 %collective-permute-start = (bf16[32,2048]{1,0:T(8,128)(2,1)S(1)}, bf16[32,2048]{1,0:T(8,128)(2,1)S(1)}, u32[]{:S(2)}, u32[]{:S(2)}) collective-permute-start(bf16[32,2048]{1,0:T(8,128)(2,1)S(1)} %get-tuple-element.155), channel_id=1, source_target_pairs={{0,8},{8,16},{16,24},{1,9},{9,17},{17,25},{2,10},{10,18},{18,26},{... | collective-permute-start | bytes 393224 | tf_op jit(solution)/shard_map/ppermute | solution.py:12
  79.2 8.7 %all-to-all-start.3 = ((s32[8,1,32]{2,1,0:T(1,128)}), s32[8,1,32]{2,1,0:T(1,128)S(1)}, u32[]{:S(2)}, u32[]{:S(2)}) async-start(s32[8,1,32]{2,1,0:T(1,128)} %all_to_all.88), calls=%async_computation.3 | async-start | bytes 8192 | tf_op jit(solution)/shard_map/all_to_all | solution.py:74
  88.0 30.1 %all-to-all-start.4 = ((bf16[8,32,2048]{2,1,0:T(8,128)(2,1)}), bf16[8,32,2048]{2,1,0:T(8,128)(2,1)S(1)}, u32[]{:S(2)}, u32[]{:S(2)}) async-start(bf16[8,32,2048]{2,1,0:T(8,128)(2,1)} %bitcast.36), calls=%async_computation.4 | async-start | bytes 2097152 | tf_op jit(solution)/shard_map/all_to_all | solution.py:73
  119.1 30.2 %all-to-all-start.5 = ((bf16[8,32,2048]{2,1,0:T(8,128)(2,1)}), bf16[8,32,2048]{2,1,0:T(8,128)(2,1)S(1)}, u32[]{:S(2)}, u32[]{:S(2)}) async-start(bf16[8,32,2048]{2,1,0:T(8,128)(2,1)} %bitcast.37), calls=%async_computation.5 | async-start | bytes 2097152 | tf_op jit(solution)/shard_map/all_to_all | solution.py:81
  151.4 7.8 %collective-permute-start.1 = (bf16[32,2048]{1,0:T(8,128)(2,1)S(1)}, bf16[32,2048]{1,0:T(8,128)(2,1)S(1)}, u32[]{:S(2)}, u32[]{:S(2)}) collective-permute-start(bf16[32,2048]{1,0:T(8,128)(2,1)S(1)} %get-tuple-element.151), channel_id=1, source_target_pairs={{0,8},{8,16},{16,24},{1,9},{9,17},{17,25},{2,10},{10,18},{18,26},{... | collective-permute-start | bytes 393224 | tf_op jit(solution)/shard_map/ppermute | solution.py:12
  153.5 8.7 %all-to-all-start.6 = ((s32[8,1,32]{2,1,0:T(1,128)}), s32[8,1,32]{2,1,0:T(1,128)S(1)}, u32[]{:S(2)}, u32[]{:S(2)}) async-start(s32[8,1,32]{2,1,0:T(1,128)} %all_to_all.92), calls=%async_computation.6 | async-start | bytes 8192 | tf_op jit(solution)/shard_map/all_to_all | solution.py:74
  162.2 30.1 %all-to-all-start.7 = ((bf16[8,32,2048]{2,1,0:T(8,128)(2,1)}), bf16[8,32,2048]{2,1,0:T(8,128)(2,1)S(1)}, u32[]{:S(2)}, u32[]{:S(2)}) async-start(bf16[8,32,2048]{2,1,0:T(8,128)(2,1)} %bitcast.52), calls=%async_computation.7 | async-start | bytes 2097152 | tf_op jit(solution)/shard_map/all_to_all | solution.py:73
  193.4 30.1 %all-to-all-start.8 = ((bf16[8,32,2048]{2,1,0:T(8,128)(2,1)}), bf16[8,32,2048]{2,1,0:T(8,128)(2,1)S(1)}, u32[]{:S(2)}, u32[]{:S(2)}) async-start(bf16[8,32,2048]{2,1,0:T(8,128)(2,1)} %bitcast.53), calls=%async_computation.8 | async-start | bytes 2097152 | tf_op jit(solution)/shard_map/all_to_all | solution.py:81
  225.4 22.4 %collective-permute-start.2 = (bf16[32,2048]{1,0:T(8,128)(2,1)S(1)}, bf16[32,2048]{1,0:T(8,128)(2,1)S(1)}, u32[]{:S(2)}, u32[]{:S(2)}) collective-permute-start(bf16[32,2048]{1,0:T(8,128)(2,1)S(1)} %get-tuple-element.147), channel_id=1, source_target_pairs={{0,8},{8,16},{16,24},{1,9},{9,17},{17,25},{2,10},{10,18},{18,26},{... | collective-permute-start | bytes 393224 | tf_op jit(solution)/shard_map/ppermute | solution.py:12
  227.5 21.9 %all-to-all-start.9 = ((s32[8,1,32]{2,1,0:T(1,128)}), s32[8,1,32]{2,1,0:T(1,128)S(1)}, u32[]{:S(2)}, u32[]{:S(2)}) async-start(s32[8,1,32]{2,1,0:T(1,128)} %all_to_all.96), calls=%async_computation.9 | async-start | bytes 8192 | tf_op jit(solution)/shard_map/all_to_all | solution.py:74
  249.5 30.1 %all-to-all-start.10 = ((bf16[8,32,2048]{2,1,0:T(8,128)(2,1)}), bf16[8,32,2048]{2,1,0:T(8,128)(2,1)S(1)}, u32[]{:S(2)}, u32[]{:S(2)}) async-start(bf16[8,32,2048]{2,1,0:T(8,128)(2,1)} %bitcast.68), calls=%async_computation.10 | async-start | bytes 2097152 | tf_op jit(solution)/shard_map/all_to_all | solution.py:73
  288.4 30.3 %all-to-all-start.11 = ((bf16[8,32,2048]{2,1,0:T(8,128)(2,1)}), bf16[8,32,2048]{2,1,0:T(8,128)(2,1)S(1)}, u32[]{:S(2)}, u32[]{:S(2)}) async-start(bf16[8,32,2048]{2,1,0:T(8,128)(2,1)} %bitcast.69), calls=%async_computation.11 | async-start | bytes 2097152 | tf_op jit(solution)/shard_map/all_to_all | solution.py:81
  320.7 9.8 %collective-permute-start.3 = (bf16[32,2048]{1,0:T(8,128)(2,1)S(1)}, bf16[32,2048]{1,0:T(8,128)(2,1)S(1)}, u32[]{:S(2)}, u32[]{:S(2)}) collective-permute-start(bf16[32,2048]{1,0:T(8,128)(2,1)S(1)} %get-tuple-element.143), channel_id=1, source_target_pairs={{0,8},{8,16},{16,24},{1,9},{9,17},{17,25},{2,10},{10,18},{18,26},{... | collective-permute-start | bytes 393224 | tf_op jit(solution)/shard_map/ppermute | solution.py:12
  322.8 9.4 %all-to-all-start.12 = ((s32[8,1,32]{2,1,0:T(1,128)}), s32[8,1,32]{2,1,0:T(1,128)S(1)}, u32[]{:S(2)}, u32[]{:S(2)}) async-start(s32[8,1,32]{2,1,0:T(1,128)} %all_to_all.100), calls=%async_computation.12 | async-start | bytes 8192 | tf_op jit(solution)/shard_map/all_to_all | solution.py:74
  332.2 30.1 %all-to-all-start.13 = ((bf16[8,32,2048]{2,1,0:T(8,128)(2,1)}), bf16[8,32,2048]{2,1,0:T(8,128)(2,1)S(1)}, u32[]{:S(2)}, u32[]{:S(2)}) async-start(bf16[8,32,2048]{2,1,0:T(8,128)(2,1)} %bitcast.84), calls=%async_computation.13 | async-start | bytes 2097152 | tf_op jit(solution)/shard_map/all_to_all | solution.py:73
  371.1 30.1 %all-to-all-start.14 = ((bf16[8,32,2048]{2,1,0:T(8,128)(2,1)}), bf16[8,32,2048]{2,1,0:T(8,128)(2,1)S(1)}, u32[]{:S(2)}, u32[]{:S(2)}) async-start(bf16[8,32,2048]{2,1,0:T(8,128)(2,1)} %bitcast.85), calls=%async_computation.14 | async-start | bytes 2097152 | tf_op jit(solution)/shard_map/all_to_all | solution.py:81
  403.2 9.8 %collective-permute-start.4 = (bf16[32,2048]{1,0:T(8,128)(2,1)S(1)}, bf16[32,2048]{1,0:T(8,128)(2,1)S(1)}, u32[]{:S(2)}, u32[]{:S(2)}) collective-permute-start(bf16[32,2048]{1,0:T(8,128)(2,1)S(1)} %get-tuple-element.139), channel_id=1, source_target_pairs={{0,8},{8,16},{16,24},{1,9},{9,17},{17,25},{2,10},{10,18},{18,26},{... | collective-permute-start | bytes 393224 | tf_op jit(solution)/shard_map/ppermute | solution.py:12
  405.3 9.4 %all-to-all-start.15 = ((s32[8,1,32]{2,1,0:T(1,128)}), s32[8,1,32]{2,1,0:T(1,128)S(1)}, u32[]{:S(2)}, u32[]{:S(2)}) async-start(s32[8,1,32]{2,1,0:T(1,128)} %all_to_all.104), calls=%async_computation.15 | async-start | bytes 8192 | tf_op jit(solution)/shard_map/all_to_all | solution.py:74
  414.7 30.1 %all-to-all-start.16 = ((bf16[8,32,2048]{2,1,0:T(8,128)(2,1)}), bf16[8,32,2048]{2,1,0:T(8,128)(2,1)S(1)}, u32[]{:S(2)}, u32[]{:S(2)}) async-start(bf16[8,32,2048]{2,1,0:T(8,128)(2,1)} %bitcast.100), calls=%async_computation.16 | async-start | bytes 2097152 | tf_op jit(solution)/shard_map/all_to_all | solution.py:73
  453.9 30.1 %all-to-all-start.17 = ((bf16[8,32,2048]{2,1,0:T(8,128)(2,1)}), bf16[8,32,2048]{2,1,0:T(8,128)(2,1)S(1)}, u32[]{:S(2)}, u32[]{:S(2)}) async-start(bf16[8,32,2048]{2,1,0:T(8,128)(2,1)} %bitcast.101), calls=%async_computation.17 | async-start | bytes 2097152 | tf_op jit(solution)/shard_map/all_to_all | solution.py:81
  485.9 9.8 %collective-permute-start.5 = (bf16[32,2048]{1,0:T(8,128)(2,1)S(1)}, bf16[32,2048]{1,0:T(8,128)(2,1)S(1)}, u32[]{:S(2)}, u32[]{:S(2)}) collective-permute-start(bf16[32,2048]{1,0:T(8,128)(2,1)S(1)} %get-tuple-element.135), channel_id=1, source_target_pairs={{0,8},{8,16},{16,24},{1,9},{9,17},{17,25},{2,10},{10,18},{18,26},{... | collective-permute-start | bytes 393224 | tf_op jit(solution)/shard_map/ppermute | solution.py:12
  488.0 9.3 %all-to-all-start.18 = ((s32[8,1,32]{2,1,0:T(1,128)}), s32[8,1,32]{2,1,0:T(1,128)S(1)}, u32[]{:S(2)}, u32[]{:S(2)}) async-start(s32[8,1,32]{2,1,0:T(1,128)} %all_to_all.108), calls=%async_computation.18 | async-start | bytes 8192 | tf_op jit(solution)/shard_map/all_to_all | solution.py:74
  497.4 30.1 %all-to-all-start.19 = ((bf16[8,32,2048]{2,1,0:T(8,128)(2,1)}), bf16[8,32,2048]{2,1,0:T(8,128)(2,1)S(1)}, u32[]{:S(2)}, u32[]{:S(2)}) async-start(bf16[8,32,2048]{2,1,0:T(8,128)(2,1)} %bitcast.117), calls=%async_computation.19 | async-start | bytes 2097152 | tf_op jit(solution)/shard_map/all_to_all | solution.py:73
  536.3 30.1 %all-to-all-start.20 = ((bf16[8,32,2048]{2,1,0:T(8,128)(2,1)}), bf16[8,32,2048]{2,1,0:T(8,128)(2,1)S(1)}, u32[]{:S(2)}, u32[]{:S(2)}) async-start(bf16[8,32,2048]{2,1,0:T(8,128)(2,1)} %bitcast.118), calls=%async_computation.20 | async-start | bytes 2097152 | tf_op jit(solution)/shard_map/all_to_all | solution.py:81
where the time goes:
time: 579 us; the launch traced here: 569 us
  waiting for transfers between devices  377 us (65%)
  starting transfers between devices  82.9 us (14%)
  matrix products  51.2 us (9%)
  local copies, waits for them, and re-layouts  37.1 us (6%)
  other arithmetic  15.1 us (3%)
  between operations  6.16 us (1%)
    all_to_all x7, waiting for transfers between devices, on_device(): lax.all_to_all(slot_buffer, 'dp', split_axis=0, concat_axis=0, tiled=True)  172 us
    all_to_all x7, waiting for transfers between devices, on_device(): lax.all_to_all(expert_out, 'dp', split_axis=0, concat_axis=0, tiled=True)  165 us
    ppermute x6, waiting for transfers between devices, shifted(): return lax.ppermute(x, axis, pairs)  34 us
    all_to_all x7, starting transfers between devices, on_device(): lax.all_to_all(expert_out, 'dp', split_axis=0, concat_axis=0, tiled=True)  25.3 us
    all_to_all x7, starting transfers between devices, on_device(): lax.all_to_all(slot_buffer, 'dp', split_axis=0, concat_axis=0, tiled=True)  25.1 us
    all_to_all x7, starting transfers between devices, on_device(): lax.all_to_all(live_slots, 'dp', split_axis=0, concat_axis=0, tiled=True)  24.7 us
    dot_general x4, matrix products, expert_rows(): jnp.dot(hidden, down_mat, preferred_element_type=jnp.float32)  24 us
  transfers between devices with their start and end apart: 27, of which 23 were waited for; matrix products, arithmetic and copies ran while one was open for 8% of the time, Pallas kernels for 0%

commit v1 on v0

--- a/solution.py
+++ b/solution.py
@@ -1,6 +1,10 @@
+import functools
+
 import jax
 import jax.numpy as jnp
 from jax import lax
+from jax.experimental import pallas as pl
+from jax.experimental.pallas import tpu as pltpu
 from jax.sharding import PartitionSpec as P
 
 EPS = 1e-06
@@ -19,7 +23,7 @@
     return jnp.dot(hidden, down_mat, preferred_element_type=jnp.float32).astype(jnp.bfloat16)
 
 
-def on_device(inputs, route, gain, router, w_gate, w_up, w_down):
+def on_device_sparse(inputs, route, gain, router, w_gate, w_up, w_down):
     section_count = lax.axis_size("section")
     section_index = lax.axis_index("section")
     micro_count, tok_rows, model_width = inputs.shape
@@ -92,7 +96,356 @@
     return states[None]
 
 
+HALF = 64
+LANES = 2 * HALF
+MESH = pl.DeviceIdType.MESH
+
+
+def relay_kernel(
+    sections, line, chunks, rows,
+    x_ref, route_ref, gain_ref, router_ref, gate_hbm, up_hbm, down_hbm, out_ref,
+    gate_v, up_v, down_v, state, gathered, part, peer_part, relay, hidden, total,
+    w_sem, x_send, x_recv, ag_send, ag_recv, ex_send, ex_recv, rs_send, rs_recv,
+):
+    sec = lax.axis_index("section")
+    dpi = lax.axis_index("dp")
+    z = dpi // 2
+    core = dpi % 2
+    width = x_ref.shape[1]
+    ff = gate_v.shape[1]
+    last = line - 1
+    has_left, has_right = z > 0, z < last
+
+    partner = (sec, z * 2 + 1 - core)
+    right = (sec, jnp.minimum(dpi + 2, 2 * line - 1))
+    left = (sec, jnp.maximum(dpi - 2, 0))
+    after = (jnp.minimum(sec + 1, sections - 1), dpi)
+    before = (jnp.maximum(sec - 1, 0), dpi)
+
+    def span(j):
+        return pl.ds(pl.multiple_of(j * rows, rows), rows)
+
+    def ag_copy(kind, j, src):
+        block = gathered.at[j, core, src]
+        return pltpu.make_async_remote_copy(
+            block, block, ag_send.at[j, kind, src], ag_recv.at[j, core, src],
+            device_id=(right, left, partner)[kind], device_id_type=MESH,
+        )
+
+    def ag_arrival(j, which, src):
+        block = gathered.at[j, which, src]
+        pltpu.make_async_remote_copy(
+            block, block, ag_send.at[j, 0, src], ag_recv.at[j, which, src],
+            device_id=partner, device_id_type=MESH,
+        ).wait_recv()
+
+    def ex_copy(j):
+        return pltpu.make_async_remote_copy(
+            part.at[j, 1 - core], peer_part.at[j], ex_send.at[j], ex_recv.at[j],
+            device_id=partner, device_id_type=MESH,
+        )
+
+    def rs_copy(way, j, dest):
+        block = relay.at[j, way, dest]
+        return pltpu.make_async_remote_copy(
+            block, block, rs_send.at[j, way, dest], rs_recv.at[j, way, dest],
+            device_id=(right, left)[way], device_id_type=MESH,
+        )
+
+    def x_copy(j):
+        return pltpu.make_async_remote_copy(
+            out_ref.at[span(j)], state.at[j], x_send.at[j], x_recv.at[j],
+            device_id=after, device_id_type=MESH,
+        )
+
+    weight_copies = [
+        pltpu.make_async_copy(gate_hbm, gate_v, w_sem.at[0]),
+        pltpu.make_async_copy(up_hbm, up_v, w_sem.at[1]),
+        pltpu.make_async_copy(down_hbm, down_v, w_sem.at[2]),
+    ]
+    for copy in weight_copies:
+        copy.start()
+
+    barrier = pltpu.get_barrier_semaphore()
+    neighbours = (
+        (None, partner),
+        (has_left, left),
+        (has_right, right),
+        (sec > 0, before),
+        (sec < sections - 1, after),
+    )
+    for cond, device in neighbours:
+        def greet(device=device):
+            pl.semaphore_signal(barrier, inc=1, device_id=device, device_id_type=MESH)
+        if cond is None:
+            greet()
+        else:
+            pl.when(cond)(greet)
+    peers = 1
+    for cond, _ in neighbours[1:]:
+        peers += jnp.where(cond, 1, 0)
+    pl.semaphore_wait(barrier, peers)
+
+    def enter(j):
+        @pl.when(sec == 0)
+        def _():
+            state[j] = x_ref[span(j)]
+
+        @pl.when(sec > 0)
+        def _():
+            x_copy(j).wait_recv()
+
+        wide = state[j].astype(jnp.float32)
+        inv_rms = lax.rsqrt(jnp.mean(wide * wide, axis=1, keepdims=True) + EPS)
+        normed = (wide * inv_rms * gain_ref[...].astype(jnp.float32)).astype(jnp.bfloat16)
+        logits = jnp.dot(normed, router_ref[...], preferred_element_type=jnp.float32)
+        lane = lax.broadcasted_iota(jnp.int32, (rows, LANES), 1)
+        folded = jnp.where(lane < HALF, lane, lane - HALF)
+        chosen = route_ref[span(j)]
+        named = folded == chosen[:, 0:1]
+        for k in range(1, chosen.shape[1]):
+            named = named | (folded == chosen[:, k:k + 1])
+        scores = jnp.where(named, jax.nn.sigmoid(logits), 0.0)
+        norm = jnp.sum(jnp.where(lane < HALF, scores, 0.0), axis=1, keepdims=True)
+        weights = scores / norm
+        high = weights.astype(jnp.bfloat16).astype(jnp.float32)
+        carried = jnp.where(lane < HALF, high, weights - high)
+        gathered[j, core, z, :, 0:width] = normed
+        gathered[j, core, z, :, width:width + LANES] = carried.astype(jnp.bfloat16)
+
+        @pl.when(has_right)
+        def _():
+            ag_copy(0, j, z).start()
+
+        @pl.when(has_left)
+        def _():
+            ag_copy(1, j, z).start()
+
+        ag_copy(2, j, z).start()
+
+    def gather_hop(hop, j):
+        @pl.when(z >= hop)
+        def _():
+            ag_arrival(j, core, z - hop)
+
+            @pl.when(has_right)
+            def _():
+                ag_copy(0, j, z - hop).start()
+
+            ag_copy(2, j, z - hop).start()
+
+        @pl.when(z + hop <= last)
+        def _():
+            ag_arrival(j, core, z + hop)
+
+            @pl.when(has_left)
+            def _():
+                ag_copy(1, j, z + hop).start()
+
+            ag_copy(2, j, z + hop).start()
+
+    def compute(j):
+        for src in range(line):
+            ag_arrival(j, 1 - core, src)
+        count = 2 * line * rows
+        block = gathered[j, :, :, :, 0:width].reshape(count, width)
+        carried = gathered[j, :, :, :, width:width + LANES].reshape(count, LANES).astype(jnp.float32)
+        lane = lax.broadcasted_iota(jnp.int32, (count, LANES), 1)
+        mine = (lane == dpi) | (lane == dpi + HALF)
+        weight = jnp.sum(jnp.where(mine, carried, 0.0), axis=1, keepdims=True)
+        step = 256
+        for lo in range(0, ff, step):
+            cols = slice(lo, lo + step)
+            gate = jnp.dot(block, gate_v[:, cols], preferred_element_type=jnp.float32)
+            up = jnp.dot(block, up_v[:, cols], preferred_element_type=jnp.float32)
+            hidden[:, cols] = (jax.nn.silu(gate) * up * weight).astype(jnp.bfloat16)
+        for lo in range(0, width, 2 * step):
+            cols = slice(lo, lo + 2 * step)
+            done = jnp.dot(hidden[...], down_v[:, cols], preferred_element_type=jnp.float32)
+            part[j, :, :, :, cols] = done.astype(jnp.bfloat16).reshape(2, line, rows, 2 * step)
+        ex_copy(j).start()
+
+    def pair_sum(j, dest):
+        return part[j, core, dest].astype(jnp.float32) + peer_part[j, dest].astype(jnp.float32)
+
+    def reduce_hop(hop, j):
+        for way in range(2):
+            place = z if way == 0 else last - z
+            dest = z + line - hop if way == 0 else z - line + hop
+
+            @pl.when(place <= hop - 1)
+            def _():
+                @pl.when(place == 0)
+                def _():
+                    relay[j, way, dest] = pair_sum(j, dest).astype(jnp.bfloat16)
+
+                @pl.when(place > 0)
+                def _():
+                    rs_copy(way, j, dest).wait_recv()
+                    held = relay[j, way, dest].astype(jnp.float32)
+                    relay[j, way, dest] = (pair_sum(j, dest) + held).astype(jnp.bfloat16)
+
+                rs_copy(way, j, dest).start()
+
+    def leave(j):
+        total[...] = state[j].astype(jnp.float32) + pair_sum(j, z)
+
+        @pl.when(has_left)
+        def _():
+            rs_copy(0, j, z).wait_recv()
+            total[...] += relay[j, 0, z].astype(jnp.float32)
+
+        @pl.when(has_right)
+        def _():
+            rs_copy(1, j, z).wait_recv()
+            total[...] += relay[j, 1, z].astype(jnp.float32)
+
+        out_ref[span(j)] = total[...].astype(jnp.bfloat16)
+
+        @pl.when(sec < sections - 1)
+        def _():
+            x_copy(j).start()
+
+    def settle(j):
+        for src in range(line):
+            @pl.when(has_right & (src <= z))
+            def _():
+                ag_copy(0, j, src).wait_send()
+
+            @pl.when(has_left & (src >= z))
+            def _():
+                ag_copy(1, j, src).wait_send()
+
+            ag_copy(2, j, src).wait_send()
+
+            @pl.when(has_right & (src > z))
+            def _():
+                rs_copy(0, j, src).wait_send()
+
+            @pl.when(has_left & (src < z))
+            def _():
+                rs_copy(1, j, src).wait_send()
+
+        ex_copy(j).wait_send()
+
+        @pl.when(sec < sections - 1)
+        def _():
+            x_copy(j).wait_send()
+
+    depth = 2 * line - 1
+
+    def round_step(r, carry):
+        def phase(late, work):
+            j = r - late
+
+            @pl.when((j >= 0) & (j < chunks))
+            def _():
+                work(j)
+
+        phase(depth, leave)
+        for hop in range(last, 0, -1):
+            def work(j, hop=hop):
+                if hop == 1:
+                    ex_copy(j).wait_recv()
+                reduce_hop(hop, j)
+            phase(last + hop, work)
+        for hop in range(last, 0, -1):
+            phase(hop, functools.partial(gather_hop, hop))
+
+        @pl.when(r == last)
+        def _():
+            for copy in weight_copies:
+                copy.wait()
+
+        phase(last, compute)
+        phase(0, enter)
+        return carry
+
+    lax.fori_loop(0, chunks + depth, round_step, 0)
+
+    def settle_step(j, carry):
+        settle(j)
+        return carry
+
+    lax.fori_loop(0, chunks, settle_step, 0)
+
+
+def on_device_dense(shape, inputs, route, gain, router, w_gate, w_up, w_down):
+    sections = shape["section"]
+    line = shape["dp"] // 2
+    micro_count, tok_rows, width = inputs.shape
+    top = route.shape[-1]
+    experts = router.shape[-1]
+    ff = w_gate.shape[-1]
+    rows = min(ROWS, tok_rows)
+    token_rows = micro_count * tok_rows
+    chunks = token_rows // rows
+    padded = jnp.pad(router[0], ((0, 0), (0, HALF - experts)))
+    router_mat = jnp.concatenate([padded, padded], axis=1)
+    bf16 = jnp.bfloat16
+    count = 2 * line * rows
+    dma = pltpu.SemaphoreType.DMA
+    vmem = pl.BlockSpec(memory_space=pltpu.VMEM)
+    far = pl.BlockSpec(memory_space=pl.ANY)
+    flops = 6 * chunks * count * width * ff
+    result = pl.pallas_call(
+        functools.partial(relay_kernel, sections, line, chunks, rows),
+        out_shape=jax.ShapeDtypeStruct((token_rows, width), bf16),
+        in_specs=[vmem] * 4 + [far] * 3,
+        out_specs=vmem,
+        scratch_shapes=[
+            pltpu.VMEM((width, ff), bf16),
+            pltpu.VMEM((width, ff), bf16),
+            pltpu.VMEM((ff, width), bf16),
+            pltpu.VMEM((chunks, rows, width), bf16),
+            pltpu.VMEM((chunks, 2, line, rows, width + LANES), bf16),
+            pltpu.VMEM((chunks, 2, line, rows, width), bf16),
+            pltpu.VMEM((chunks, line, rows, width), bf16),
+            pltpu.VMEM((chunks, 2, line, rows, width), bf16),
+            pltpu.VMEM((count, ff), bf16),
+            pltpu.VMEM((rows, width), jnp.float32),
+            dma((3,)),
+            dma((chunks,)),
+            dma((chunks,)),
+            dma((chunks, 3, line)),
+            dma((chunks, 2, line)),
+            dma((chunks,)),
+            dma((chunks,)),
+            dma((chunks, 2, line)),
+            dma((chunks, 2, line)),
+        ],
+        compiler_params=pltpu.CompilerParams(
+            collective_id=0, has_side_effects=True, vmem_limit_bytes=56 * 2**20
+        ),
+        cost_estimate=pl.CostEstimate(
+            flops=flops, bytes_accessed=6 * width * ff, transcendentals=chunks * count * ff
+        ),
+    )(
+        inputs.reshape(token_rows, width),
+        route.reshape(token_rows, top),
+        gain,
+        router_mat,
+        w_gate[0, 0],
+        w_up[0, 0],
+        w_down[0, 0],
+    )
+    return result.reshape(1, micro_count, tok_rows, width)
+
+
+ROWS = 16
+
+
+def on_device(shape, inputs, route, gain, router, w_gate, w_up, w_down):
+    tok_rows = inputs.shape[1]
+    experts = router.shape[-1]
+    args = (inputs, route, gain, router, w_gate, w_up, w_down)
+    if 2 * tok_rows * route.shape[-1] // experts >= tok_rows and experts <= HALF:
+        return on_device_dense(shape, *args)
+    return on_device_sparse(*args)
+
+
 def solution(mesh):
+    body = functools.partial(on_device, dict(mesh.shape))
     in_specs = (
         P(None, "dp", None),
         P("section", None, "dp", None),
@@ -104,5 +457,5 @@
     )
     out_specs = P("section", None, "dp", None)
     return jax.shard_map(
-        on_device, mesh=mesh, in_specs=in_specs, out_specs=out_specs, check_vma=False
+        body, mesh=mesh, in_specs=in_specs, out_specs=out_specs, check_vma=False
     )

time: 579 us -> 190 us (0.33); the launches traced: 569 us -> 190 us
  waiting for transfers between devices: 377 us -> 0 us
  Pallas kernels: 0 us -> 184 us
  starting transfers between devices: 82.9 us -> 0 us
  matrix products: 51.2 us -> 0 us
  local copies, waits for them, and re-layouts: 37.1 us -> 4.44 us
  other arithmetic: 15.1 us -> 1.08 us
  between operations: 6.16 us -> 0.02 us
    all_to_all x21 -> x0, waiting for transfers between devices: 343 us -> none  [the longest x7 172 us: on_device(): lax.all_to_all(slot_buffer, 'dp', split_axis=0, concat_axis=0, tiled=True)]
    pallas_call x0 -> x1, Pallas kernels: none -> 184 us  [on_device_dense(): pl.pallas_call(functools.partial(relay_kernel, sections, line, chunks, ro...]
    all_to_all x21 -> x0, starting transfers between devices: 75.1 us -> none  [the longest x7 25.3 us: on_device(): lax.all_to_all(expert_out, 'dp', split_axis=0, concat_axis=0, tiled=True)]
    dot_general x29 -> x0, matrix products: 51.2 us -> none  [the longest x4 24 us: expert_rows(): jnp.dot(hidden, down_mat, preferred_element_type=jnp.float32)]
    ppermute x6 -> x0, waiting for transfers between devices: 34 us -> none  [shifted(): return lax.ppermute(x, axis, pairs)]
    gather x42 -> x0, local copies, waits for them, and re-layouts: 19.1 us -> none  [the longest x35 11.1 us: on_device(): scores = jax.nn.sigmoid(jnp.take_along_axis(logits, chosen_ids, axis=1))]
    ppermute x6 -> x0, starting transfers between devices: 7.75 us -> none  [shifted(): return lax.ppermute(x, axis, pairs)]
  transfers between devices with their start and end apart: 27 -> 0, of which waited for: 23 -> 0; matrix products, arithmetic and copies ran while one was open for 8% -> 0% of each run, Pallas kernels for 0% -> 0%
where the time goes in v1:
time: 190 us
  Pallas kernels  184 us (97%)
  local copies, waits for them, and re-layouts  4.44 us (2%)
    pallas_call x1, Pallas kernels, on_device_dense(): pl.pallas_call(functools.partial(relay_kernel, sections, line, chunks, ro...  184 us
    unnamed x3, local copies, waits for them, and re-layouts  4.33 us

profile of v1, /device:TPU:6, one launch (start us, length us, event | category | flops | bytes accessed | tf_op | source)
XLA Modules:
  0.0 189.9 jit_solution(3075770338600990733)
XLA Ops:
  0.0 1.4 copy.8
  1.4 1.0 copy.9
  2.5 0.1 pad.4
  2.6 1.1 pad_maximum_fusion.router_ref
  3.7 184.3 %shard_map.73 = bf16[128,2048]{1,0:T(8,128)(2,1)} custom-call(bf16[128,2048]{1,0:T(8,128)(2,1)} %bitcast.13, s32[128,6]{1,0:T(8,128)} %bitcast.9, bf16[1,2048]{1,0:T(2,128)(2,1)} %gain_ref.1, bf16[2048,128]{1,0:T(8,128)(2,1)} %pad_maximum_fusion.router_ref, bf16[2048,768]{1,0:T(8,128)(2,1)} %bitcast.10, bf16[2048,768]{1,0:T(8,128)(2,1)} %bitcast.11, ...), custom_call_target="tpu_custom_call" | custom-call | flops 9663676416 | bytes 9437184 | tf_op jit(solution)/shard_map/pallas_call | solution.py:391
  188.0 1.9 copy.11

commit v2 on v1

--- a/solution.py
+++ b/solution.py
@@ -98,14 +98,16 @@
 
 HALF = 64
 LANES = 2 * HALF
+SLICE = 512
 MESH = pl.DeviceIdType.MESH
 
 
 def relay_kernel(
     sections, line, chunks, rows,
     x_ref, route_ref, gain_ref, router_ref, gate_hbm, up_hbm, down_hbm, out_ref,
-    gate_v, up_v, down_v, state, gathered, part, peer_part, relay, hidden, total,
-    w_sem, x_send, x_recv, ag_send, ag_recv, ex_send, ex_recv, rs_send, rs_recv,
+    gate_v, up_v, down_v, state, gathered, part, peer_part, stage, near_in, far_in, hidden,
+    w_sem, x_send, x_recv, mate_send, cross_send, pair_send, ag_recv, ex_send, ex_recv,
+    near_send, near_recv, far_send, far_recv,
 ):
     sec = lax.axis_index("section")
     dpi = lax.axis_index("dp")
@@ -113,44 +115,58 @@
     core = dpi % 2
     width = x_ref.shape[1]
     ff = gate_v.shape[1]
-    last = line - 1
-    has_left, has_right = z > 0, z < last
+    low_half = z < 2
+    inner = (z == 1) | (z == 2)
+    mate_z = z + 1 - 2 * (z % 2)
+    cross_z = jnp.where(low_half, 2, 1)
+    edge_z = jnp.where(low_half, 3, 0)
 
     partner = (sec, z * 2 + 1 - core)
-    right = (sec, jnp.minimum(dpi + 2, 2 * line - 1))
-    left = (sec, jnp.maximum(dpi - 2, 0))
+    mate = (sec, mate_z * 2 + core)
+    cross = (sec, cross_z * 2 + core)
+    edge = (sec, edge_z * 2 + core)
     after = (jnp.minimum(sec + 1, sections - 1), dpi)
     before = (jnp.maximum(sec - 1, 0), dpi)
 
     def span(j):
         return pl.ds(pl.multiple_of(j * rows, rows), rows)
 
-    def ag_copy(kind, j, src):
+    def remote(src, dst, send, recv, device):
+        return pltpu.make_async_remote_copy(
+            src, dst, send, recv, device_id=device, device_id_type=MESH
+        )
+
+    def to_mate(j, src):
         block = gathered.at[j, core, src]
-        return pltpu.make_async_remote_copy(
-            block, block, ag_send.at[j, kind, src], ag_recv.at[j, core, src],
-            device_id=(right, left, partner)[kind], device_id_type=MESH,
-        )
+        return remote(block, block, mate_send.at[j, src], ag_recv.at[j, core, src], mate)
+
+    def to_cross(j):
+        block = gathered.at[j, core, z]
+        return remote(block, block, cross_send.at[j], ag_recv.at[j, core, z], cross)
+
+    def to_partner(j, src):
+        block = gathered.at[j, core, src]
+        return remote(block, block, pair_send.at[j, src], ag_recv.at[j, core, src], partner)
 
     def ag_arrival(j, which, src):
         block = gathered.at[j, which, src]
-        pltpu.make_async_remote_copy(
-            block, block, ag_send.at[j, 0, src], ag_recv.at[j, which, src],
-            device_id=partner, device_id_type=MESH,
-        ).wait_recv()
-
-    def ex_copy(j):
-        return pltpu.make_async_remote_copy(
-            part.at[j, 1 - core], peer_part.at[j], ex_send.at[j], ex_recv.at[j],
-            device_id=partner, device_id_type=MESH,
-        )
-
-    def rs_copy(way, j, dest):
-        block = relay.at[j, way, dest]
-        return pltpu.make_async_remote_copy(
-            block, block, rs_send.at[j, way, dest], rs_recv.at[j, way, dest],
-            device_id=(right, left)[way], device_id_type=MESH,
-        )
+        remote(block, block, pair_send.at[j, src], ag_recv.at[j, which, src], partner).wait_recv()
+
+    def ex_copy(j, piece):
+        cols = pl.ds(piece * SLICE, SLICE)
+        return remote(
+            part.at[j, 1 - core, :, :, cols], peer_part.at[j, :, :, cols],
+            ex_send.at[j, piece], ex_recv.at[j, piece], partner,
+        )
+
+    def near_copy(j, dest):
+        return remote(
+            stage.at[j, dest], near_in.at[j, dest], near_send.at[j, dest], near_recv.at[j, dest], mate
+        )
+
+    def far_copy(j, which):
+        dest, device = ((cross_z, cross), (edge_z, edge))[which]
+        return remote(stage.at[j, dest], far_in.at[j], far_send.at[j, which], far_recv.at[j], device)
 
     def x_copy(j):
         return pltpu.make_async_remote_copy(
@@ -169,8 +185,9 @@
     barrier = pltpu.get_barrier_semaphore()
     neighbours = (
         (None, partner),
-        (has_left, left),
-        (has_right, right),
+        (None, mate),
+        (None, cross),
+        (inner, edge),
         (sec > 0, before),
         (sec < sections - 1, after),
     )
@@ -181,8 +198,8 @@
             greet()
         else:
             pl.when(cond)(greet)
-    peers = 1
-    for cond, _ in neighbours[1:]:
+    peers = 3
+    for cond, _ in neighbours[3:]:
         peers += jnp.where(cond, 1, 0)
     pl.semaphore_wait(barrier, peers)
 
@@ -213,36 +230,27 @@
         gathered[j, core, z, :, 0:width] = normed
         gathered[j, core, z, :, width:width + LANES] = carried.astype(jnp.bfloat16)
 
-        @pl.when(has_right)
-        def _():
-            ag_copy(0, j, z).start()
-
-        @pl.when(has_left)
-        def _():
-            ag_copy(1, j, z).start()
-
-        ag_copy(2, j, z).start()
-
-    def gather_hop(hop, j):
-        @pl.when(z >= hop)
-        def _():
-            ag_arrival(j, core, z - hop)
-
-            @pl.when(has_right)
-            def _():
-                ag_copy(0, j, z - hop).start()
-
-            ag_copy(2, j, z - hop).start()
-
-        @pl.when(z + hop <= last)
-        def _():
-            ag_arrival(j, core, z + hop)
-
-            @pl.when(has_left)
-            def _():
-                ag_copy(1, j, z + hop).start()
-
-            ag_copy(2, j, z + hop).start()
+        to_cross(j).start()
+        to_mate(j, z).start()
+        to_partner(j, z).start()
+
+    def gather_near(j):
+        @pl.when(inner)
+        def _():
+            for src in (cross_z, edge_z):
+                ag_arrival(j, core, src)
+                to_mate(j, src).start()
+                to_partner(j, src).start()
+
+        ag_arrival(j, core, mate_z)
+        to_partner(j, mate_z).start()
+
+    def gather_far(j):
+        @pl.when(jnp.logical_not(inner))
+        def _():
+            for src in (cross_z, edge_z):
+                ag_arrival(j, core, src)
+                to_partner(j, src).start()
 
     def compute(j):
         for src in range(line):
@@ -259,80 +267,73 @@
             gate = jnp.dot(block, gate_v[:, cols], preferred_element_type=jnp.float32)
             up = jnp.dot(block, up_v[:, cols], preferred_element_type=jnp.float32)
             hidden[:, cols] = (jax.nn.silu(gate) * up * weight).astype(jnp.bfloat16)
-        for lo in range(0, width, 2 * step):
-            cols = slice(lo, lo + 2 * step)
+        for piece in range(width // SLICE):
+            cols = slice(piece * SLICE, piece * SLICE + SLICE)
             done = jnp.dot(hidden[...], down_v[:, cols], preferred_element_type=jnp.float32)
-            part[j, :, :, :, cols] = done.astype(jnp.bfloat16).reshape(2, line, rows, 2 * step)
-        ex_copy(j).start()
+            part[j, :, :, :, cols] = done.astype(jnp.bfloat16).reshape(2, line, rows, SLICE)
+            ex_copy(j, piece).start()
 
     def pair_sum(j, dest):
         return part[j, core, dest].astype(jnp.float32) + peer_part[j, dest].astype(jnp.float32)
 
-    def reduce_hop(hop, j):
-        for way in range(2):
-            place = z if way == 0 else last - z
-            dest = z + line - hop if way == 0 else z - line + hop
-
-            @pl.when(place <= hop - 1)
-            def _():
-                @pl.when(place == 0)
-                def _():
-                    relay[j, way, dest] = pair_sum(j, dest).astype(jnp.bfloat16)
-
-                @pl.when(place > 0)
-                def _():
-                    rs_copy(way, j, dest).wait_recv()
-                    held = relay[j, way, dest].astype(jnp.float32)
-                    relay[j, way, dest] = (pair_sum(j, dest) + held).astype(jnp.bfloat16)
-
-                rs_copy(way, j, dest).start()
+    def reduce_near(j):
+        for piece in range(width // SLICE):
+            ex_copy(j, piece).wait_recv()
+
+        @pl.when(jnp.logical_not(inner))
+        def _():
+            for dest in (edge_z, cross_z):
+                stage[j, dest] = pair_sum(j, dest).astype(jnp.bfloat16)
+                near_copy(j, dest).start()
+
+        stage[j, mate_z] = pair_sum(j, mate_z).astype(jnp.bfloat16)
+        near_copy(j, mate_z).start()
+
+    def reduce_far(j):
+        @pl.when(inner)
+        def _():
+            for which, dest in ((1, edge_z), (0, cross_z)):
+                near_copy(j, dest).wait_recv()
+                held = near_in[j, dest].astype(jnp.float32)
+                stage[j, dest] = (pair_sum(j, dest) + held).astype(jnp.bfloat16)
+                far_copy(j, which).start()
 
     def leave(j):
-        total[...] = state[j].astype(jnp.float32) + pair_sum(j, z)
-
-        @pl.when(has_left)
-        def _():
-            rs_copy(0, j, z).wait_recv()
-            total[...] += relay[j, 0, z].astype(jnp.float32)
-
-        @pl.when(has_right)
-        def _():
-            rs_copy(1, j, z).wait_recv()
-            total[...] += relay[j, 1, z].astype(jnp.float32)
-
-        out_ref[span(j)] = total[...].astype(jnp.bfloat16)
+        near_copy(j, z).wait_recv()
+        far_copy(j, 0).wait_recv()
+        held = near_in[j, z].astype(jnp.float32) + far_in[j].astype(jnp.float32)
+        total = state[j].astype(jnp.float32) + (pair_sum(j, z) + held)
+        out_ref[span(j)] = total.astype(jnp.bfloat16)
 
         @pl.when(sec < sections - 1)
         def _():
             x_copy(j).start()
 
     def settle(j):
+        to_cross(j).wait_send()
+        to_mate(j, z).wait_send()
         for src in range(line):
-            @pl.when(has_right & (src <= z))
-            def _():
-                ag_copy(0, j, src).wait_send()
-
-            @pl.when(has_left & (src >= z))
-            def _():
-                ag_copy(1, j, src).wait_send()
-
-            ag_copy(2, j, src).wait_send()
-
-            @pl.when(has_right & (src > z))
-            def _():
-                rs_copy(0, j, src).wait_send()
-
-            @pl.when(has_left & (src < z))
-            def _():
-                rs_copy(1, j, src).wait_send()
-
-        ex_copy(j).wait_send()
+            to_partner(j, src).wait_send()
+        for piece in range(width // SLICE):
+            ex_copy(j, piece).wait_send()
+        near_copy(j, mate_z).wait_send()
+
+        @pl.when(inner)
+        def _():
+            for which, src in ((1, edge_z), (0, cross_z)):
+                to_mate(j, src).wait_send()
+                far_copy(j, which).wait_send()
+
+        @pl.when(jnp.logical_not(inner))
+        def _():
+            for dest in (edge_z, cross_z):
+                near_copy(j, dest).wait_send()
 
         @pl.when(sec < sections - 1)
         def _():
             x_copy(j).wait_send()
 
-    depth = 2 * line - 1
+    depth = 5
 
     def round_step(r, carry):
         def phase(late, work):
@@ -342,23 +343,19 @@
             def _():
                 work(j)
 
-        phase(depth, leave)
-        for hop in range(last, 0, -1):
-            def work(j, hop=hop):
-                if hop == 1:
-                    ex_copy(j).wait_recv()
-                reduce_hop(hop, j)
-            phase(last + hop, work)
-        for hop in range(last, 0, -1):
-            phase(hop, functools.partial(gather_hop, hop))
-
-        @pl.when(r == last)
+        phase(2, gather_far)
+        phase(1, gather_near)
+        phase(5, leave)
+        phase(4, reduce_far)
+        phase(3, reduce_near)
+        phase(0, enter)
+
+        @pl.when(r == 2)
         def _():
             for copy in weight_copies:
                 copy.wait()
 
-        phase(last, compute)
-        phase(0, enter)
+        phase(2, compute)
         return carry
 
     lax.fori_loop(0, chunks + depth, round_step, 0)
@@ -401,18 +398,23 @@
             pltpu.VMEM((chunks, 2, line, rows, width + LANES), bf16),
             pltpu.VMEM((chunks, 2, line, rows, width), bf16),
             pltpu.VMEM((chunks, line, rows, width), bf16),
-            pltpu.VMEM((chunks, 2, line, rows, width), bf16),
+            pltpu.VMEM((chunks, line, rows, width), bf16),
+            pltpu.VMEM((chunks, line, rows, width), bf16),
+            pltpu.VMEM((chunks, rows, width), bf16),
             pltpu.VMEM((count, ff), bf16),
-            pltpu.VMEM((rows, width), jnp.float32),
             dma((3,)),
             dma((chunks,)),
             dma((chunks,)),
-            dma((chunks, 3, line)),
+            dma((chunks, line)),
+            dma((chunks,)),
+            dma((chunks, line)),
             dma((chunks, 2, line)),
+            dma((chunks, width // SLICE)),
+            dma((chunks, width // SLICE)),
+            dma((chunks, line)),
+            dma((chunks, line)),
+            dma((chunks, 2)),
             dma((chunks,)),
-            dma((chunks,)),
-            dma((chunks, 2, line)),
-            dma((chunks, 2, line)),
         ],
         compiler_params=pltpu.CompilerParams(
             collective_id=0, has_side_effects=True, vmem_limit_bytes=56 * 2**20
@@ -439,7 +441,7 @@
     tok_rows = inputs.shape[1]
     experts = router.shape[-1]
     args = (inputs, route, gain, router, w_gate, w_up, w_down)
-    if 2 * tok_rows * route.shape[-1] // experts >= tok_rows and experts <= HALF:
+    if 2 * tok_rows * route.shape[-1] // experts >= tok_rows and experts <= HALF and shape["dp"] == 8:
         return on_device_dense(shape, *args)
     return on_device_sparse(*args)
 

time: 190 us -> 210 us (1.11); the launches traced: 190 us -> 208 us
  Pallas kernels: 184 us -> 202 us
    pallas_call x1, Pallas kernels: 184 us -> 202 us  [on_device_dense(): pl.pallas_call(functools.partial(relay_kernel, sections, line, chunks, ro...]
where the time goes in v2:
time: 210 us; the launch traced here: 208 us
  Pallas kernels  202 us (96%)
  local copies, waits for them, and re-layouts  4.44 us (2%)
    pallas_call x1, Pallas kernels, on_device_dense(): pl.pallas_call(functools.partial(relay_kernel, sections, line, chunks, ro...  202 us
    unnamed x3, local copies, waits for them, and re-layouts  4.33 us

profile of v2, /device:TPU:6, one launch (start us, length us, event | category | flops | bytes accessed | tf_op | source)
XLA Modules:
  0.0 207.5 jit_solution(15398254408365121217)
XLA Ops:
  0.0 1.4 copy.8
  1.4 1.0 copy.9
  2.5 0.1 pad.4
  2.6 1.1 pad_maximum_fusion.router_ref
  3.7 202.0 %shard_map.73 = bf16[128,2048]{1,0:T(8,128)(2,1)} custom-call(bf16[128,2048]{1,0:T(8,128)(2,1)} %bitcast.13, s32[128,6]{1,0:T(8,128)} %bitcast.9, bf16[1,2048]{1,0:T(2,128)(2,1)} %gain_ref.1, bf16[2048,128]{1,0:T(8,128)(2,1)} %pad_maximum_fusion.router_ref, bf16[2048,768]{1,0:T(8,128)(2,1)} %bitcast.10, bf16[2048,768]{1,0:T(8,128)(2,1)} %bitcast.11, ...), custom_call_target="tpu_custom_call" | custom-call | flops 9663676416 | bytes 9437184 | tf_op jit(solution)/shard_map/pallas_call | solution.py:388
  205.6 1.9 copy.11

commit v3 on v1

--- a/solution.py
+++ b/solution.py
@@ -98,6 +98,8 @@
 
 HALF = 64
 LANES = 2 * HALF
+SLICE = 512
+STRIDE = 3
 MESH = pl.DeviceIdType.MESH
 
 
@@ -113,6 +115,7 @@
     core = dpi % 2
     width = x_ref.shape[1]
     ff = gate_v.shape[1]
+    pieces = width // SLICE
     last = line - 1
     has_left, has_right = z > 0, z < last
 
@@ -139,9 +142,11 @@
             device_id=partner, device_id_type=MESH,
         ).wait_recv()
 
-    def ex_copy(j):
+    def ex_copy(j, piece):
+        cols = pl.ds(piece * SLICE, SLICE)
         return pltpu.make_async_remote_copy(
-            part.at[j, 1 - core], peer_part.at[j], ex_send.at[j], ex_recv.at[j],
+            part.at[j, 1 - core, :, :, cols], peer_part.at[j, :, :, cols],
+            ex_send.at[j, piece], ex_recv.at[j, piece],
             device_id=partner, device_id_type=MESH,
         )
 
@@ -259,11 +264,11 @@
             gate = jnp.dot(block, gate_v[:, cols], preferred_element_type=jnp.float32)
             up = jnp.dot(block, up_v[:, cols], preferred_element_type=jnp.float32)
             hidden[:, cols] = (jax.nn.silu(gate) * up * weight).astype(jnp.bfloat16)
-        for lo in range(0, width, 2 * step):
-            cols = slice(lo, lo + 2 * step)
+        for piece in range(pieces):
+            cols = slice(piece * SLICE, piece * SLICE + SLICE)
             done = jnp.dot(hidden[...], down_v[:, cols], preferred_element_type=jnp.float32)
-            part[j, :, :, :, cols] = done.astype(jnp.bfloat16).reshape(2, line, rows, 2 * step)
-        ex_copy(j).start()
+            part[j, :, :, :, cols] = done.astype(jnp.bfloat16).reshape(2, line, rows, SLICE)
+            ex_copy(j, piece).start()
 
     def pair_sum(j, dest):
         return part[j, core, dest].astype(jnp.float32) + peer_part[j, dest].astype(jnp.float32)
@@ -326,7 +331,8 @@
             def _():
                 rs_copy(1, j, src).wait_send()
 
-        ex_copy(j).wait_send()
+        for piece in range(pieces):
+            ex_copy(j, piece).wait_send()
 
         @pl.when(sec < sections - 1)
         def _():
@@ -336,21 +342,25 @@
 
     def round_step(r, carry):
         def phase(late, work):
-            j = r - late
-
-            @pl.when((j >= 0) & (j < chunks))
+            past = r - late
+            j = past // STRIDE
+
+            @pl.when((past >= 0) & (past % STRIDE == 0) & (j < chunks))
             def _():
                 work(j)
+
+        def reduce_first(j):
+            for piece in range(pieces):
+                ex_copy(j, piece).wait_recv()
+            reduce_hop(1, j)
 
         phase(depth, leave)
         for hop in range(last, 0, -1):
-            def work(j, hop=hop):
-                if hop == 1:
-                    ex_copy(j).wait_recv()
-                reduce_hop(hop, j)
-            phase(last + hop, work)
-        for hop in range(last, 0, -1):
             phase(hop, functools.partial(gather_hop, hop))
+        for hop in range(last, 1, -1):
+            phase(last + hop, functools.partial(reduce_hop, hop))
+        phase(last + 1, reduce_first)
+        phase(0, enter)
 
         @pl.when(r == last)
         def _():
@@ -358,16 +368,10 @@
                 copy.wait()
 
         phase(last, compute)
-        phase(0, enter)
+        phase(depth + 2, settle)
         return carry
 
-    lax.fori_loop(0, chunks + depth, round_step, 0)
-
-    def settle_step(j, carry):
-        settle(j)
-        return carry
-
-    lax.fori_loop(0, chunks, settle_step, 0)
+    lax.fori_loop(0, (chunks - 1) * STRIDE + depth + 3, round_step, 0)
 
 
 def on_device_dense(shape, inputs, route, gain, router, w_gate, w_up, w_down):
@@ -409,8 +413,8 @@
             dma((chunks,)),
             dma((chunks, 3, line)),
             dma((chunks, 2, line)),
-            dma((chunks,)),
-            dma((chunks,)),
+            dma((chunks, width // SLICE)),
+            dma((chunks, width // SLICE)),
             dma((chunks, 2, line)),
             dma((chunks, 2, line)),
         ],

time: 190 us -> 210 us (1.11)
  Pallas kernels: 184 us -> 204 us
    pallas_call x1, Pallas kernels: 184 us -> 204 us  [on_device_dense(): pl.pallas_call(functools.partial(relay_kernel, sections, line, chunks, ro...]
where the time goes in v3:
time: 210 us
  Pallas kernels  204 us (97%)
  local copies, waits for them, and re-layouts  4.44 us (2%)
    pallas_call x1, Pallas kernels, on_device_dense(): pl.pallas_call(functools.partial(relay_kernel, sections, line, chunks, ro...  204 us
    unnamed x3, local copies, waits for them, and re-layouts  4.33 us

profile of v3, /device:TPU:6, one launch (start us, length us, event | category | flops | bytes accessed | tf_op | source)
XLA Modules:
  0.0 209.5 jit_solution(8715801957022591687)
XLA Ops:
  0.0 1.4 copy.8
  1.4 1.0 copy.9
  2.5 0.1 pad.4
  2.6 1.1 pad_maximum_fusion.router_ref
  3.7 204.0 %shard_map.73 = bf16[128,2048]{1,0:T(8,128)(2,1)} custom-call(bf16[128,2048]{1,0:T(8,128)(2,1)} %bitcast.13, s32[128,6]{1,0:T(8,128)} %bitcast.9, bf16[1,2048]{1,0:T(2,128)(2,1)} %gain_ref.1, bf16[2048,128]{1,0:T(8,128)(2,1)} %pad_maximum_fusion.router_ref, bf16[2048,768]{1,0:T(8,128)(2,1)} %bitcast.10, bf16[2048,768]{1,0:T(8,128)(2,1)} %bitcast.11, ...), custom_call_target="tpu_custom_call" | custom-call | flops 9663676416 | bytes 9437184 | tf_op jit(solution)/shard_map/pallas_call | solution.py:395
  207.7 1.9 copy.11
